TPU v7x, 32 devices: a whole 2x2x4 slice. The times are simulated.
32 devices in a mesh: pipe: 4 (over y, core), seq: 4 (over z), tp: 2 (over x).
Axes of the slice: x: 2, y: 2, z: 4, core: 2. Of those that a mesh axis runs over, the one named last changes fastest.
Arguments:
- upstream: bfloat16 [4, 2, 384, 2048], P('pipe', 'tp', 'seq'), may hold values from -6 to 6
- queries: bfloat16 [4, 2, 384, 2048], P('pipe', 'tp', 'seq'), may hold values from -6 to 6
- attention_out: bfloat16 [4, 2, 384, 2048], P('pipe', 'tp', 'seq'), may hold values from -6 to 6
- keys_values: bfloat16 [4, 2, 32, 384, 128], P('pipe', 'tp', 'seq'), may hold values from -6 to 6
- log_totals: float32 [4, 2, 32, 384], P('pipe', 'tp', 'seq'), may hold values from 3.5 to 5.5
- neighbours: int32 [12, 7], replicated, may hold values from -1 to 11, as said below
Outputs:
- query_grad: bfloat16 [4, 2, 32, 384, 64], P('pipe', 'tp', 'seq')
- cache_grad: bfloat16 [4, 2, 32, 384, 128], P('pipe', 'tp', 'seq')
Inputs may be any that keep to these rules, and one draw needn't show every extreme that they name: `neighbours`: in each row the used entries come first and are distinct; the first is the row's own block; every used entry lies within 4 blocks of the row's block; unused entries are -1. Some aligned run of 6 rows has every row listing as many blocks as lie within reach, up to 7; elsewhere rows list 1 to 3 blocks.
All inputs are finite; a program needn't handle non-finite values.
Results may differ from a plain program's by a relative error of at most 0.0055.
Values may be sent and summed in bfloat16 or wider, within the bound.
A program may use at most 128 MiB of HBM per device.

v0:
```python
import jax
import jax.numpy as jnp
from jax import lax
from jax.sharding import PartitionSpec as P

H = 32
HD = 64
BLK = 64
REACH = 4
NBR = 7


pair_group = 32


def passed_along(value, axis, steps):
    count = lax.axis_size(axis)
    pairs = [(source, (source + steps) % count) for source in range(count)]
    return lax.ppermute(value, axis, pairs)


def padded_2(cells, sides, width):
    for axis, dim in sides:
        count = lax.axis_size(axis)
        ends = count - 1
        head = lax.slice_in_dim(cells, 0, width, axis=dim)
        tail = lax.slice_in_dim(cells, cells.shape[dim] - width, cells.shape[dim], axis=dim)
        cells = jnp.concatenate(
            [
                lax.ppermute(tail, axis, [(i, (i + 1) % count) for i in range(ends)]),
                cells,
                lax.ppermute(head, axis, [((i + 1) % count, i) for i in range(ends)]),
            ],
            axis=dim,
        )
    return cells


def block_layout(values, blocks_here):
    heads_here = values.shape[1]
    turned = jnp.transpose(values, (1, 0, 2))
    return turned.reshape(heads_here, blocks_here, BLK, values.shape[2])


def body(upstream, queries, attention_out, keys_values, log_totals, neighbours):
    tokens_here = queries.shape[2]
    inv_root = HD ** (-0.5)
    incoming = passed_along(upstream, "pipe", -1)
    query_tok = queries.reshape(tokens_here, H, HD)
    grad_tok = incoming.reshape(tokens_here, H, HD)
    out_tok = attention_out.reshape(tokens_here, H, HD)
    packed = jnp.concatenate([query_tok, grad_tok, out_tok], axis=2)
    regrouped = lax.all_to_all(packed, "seq", split_axis=1, concat_axis=0, tiled=True)
    query_heads = regrouped[:, :, :HD]
    grad_heads = regrouped[:, :, HD : 2 * HD]
    out_heads = regrouped[:, :, 2 * HD :]
    row_delta = jnp.sum(grad_heads.astype(jnp.float32) * out_heads.astype(jnp.float32), axis=2)
    rows_here = query_heads.shape[0]
    heads_here = query_heads.shape[1]
    blocks_here = rows_here // BLK
    query_blocks = block_layout(query_heads, blocks_here)
    grad_blocks = block_layout(grad_heads, blocks_here)
    delta_blocks = jnp.transpose(row_delta).reshape(heads_here, blocks_here, BLK)
    norm_blocks = log_totals.reshape(heads_here, blocks_here, BLK)
    cache_blocks = keys_values.reshape(heads_here, blocks_here, BLK, 2 * HD)
    padded = padded_2(cache_blocks, (("tp", 1),), REACH)
    first_block = lax.axis_index("tp") * blocks_here
    listed = lax.dynamic_slice_in_dim(neighbours, first_block, blocks_here, 0)
    present = (listed >= 0).reshape(-1)
    slot_count = blocks_here * NBR
    group_total = (slot_count + pair_group - 1) // pair_group
    capacity = group_total * pair_group
    running = jnp.cumsum(present.astype(jnp.int32)) - 1
    pair_count = jnp.sum(present.astype(jnp.int32))
    target = jnp.where(present, running, capacity)
    query_source = jnp.repeat(jnp.arange(blocks_here, dtype=jnp.int32), NBR)
    key_source = (listed - first_block + REACH).reshape(-1)
    pair_query = jnp.zeros((capacity,), jnp.int32).at[target].set(query_source, mode="drop")
    pair_key = jnp.zeros((capacity,), jnp.int32).at[target].set(key_source, mode="drop")

    def one_group(group_step, totals):
        query_acc, cache_acc = totals
        first_pair = group_step * pair_group
        query_pick = lax.dynamic_slice_in_dim(pair_query, first_pair, pair_group)
        key_pick = lax.dynamic_slice_in_dim(pair_key, first_pair, pair_group)
        live_mask = (first_pair + jnp.arange(pair_group) < pair_count).astype(jnp.float32)
        query_rows = query_blocks[:, query_pick]
        grad_rows = grad_blocks[:, query_pick]
        norm_rows = norm_blocks[:, query_pick]
        delta_rows = delta_blocks[:, query_pick]
        cache_rows = padded[:, key_pick]
        key_rows = cache_rows[..., :HD]
        value_rows = cache_rows[..., HD:]
        scores = (
            jnp.einsum("hgqd,hgkd->hgqk", query_rows, key_rows, preferred_element_type=jnp.float32)
            * inv_root
        )
        weights = jnp.exp(scores - norm_rows[..., None]) * live_mask[None, :, None, None]
        weights_half = weights.astype(jnp.bfloat16)
        grad_weights = jnp.einsum(
            "hgqd,hgkd->hgqk", grad_rows, value_rows, preferred_element_type=jnp.float32
        )
        grad_scores = (weights * (grad_weights - delta_rows[..., None])).astype(jnp.bfloat16)
        query_part = (
            jnp.einsum("hgqk,hgkd->hgqd", grad_scores, key_rows, preferred_element_type=jnp.float32)
            * inv_root
        )
        key_part = (
            jnp.einsum(
                "hgqk,hgqd->hgkd", grad_scores, query_rows, preferred_element_type=jnp.float32
            )
            * inv_root
        )
        value_part = jnp.einsum(
            "hgqk,hgqd->hgkd", weights_half, grad_rows, preferred_element_type=jnp.float32
        )
        query_acc = query_acc.at[:, query_pick].add(query_part)
        cache_acc = cache_acc.at[:, key_pick].add(jnp.concatenate([key_part, value_part], axis=-1))
        return (query_acc, cache_acc)

    group_live = (pair_count + pair_group - 1) // pair_group
    query_start = jnp.zeros((heads_here, blocks_here, BLK, HD), jnp.float32)
    cache_start = jnp.zeros((heads_here, blocks_here + 2 * REACH, BLK, 2 * HD), jnp.float32)
    query_acc, cache_acc = lax.fori_loop(0, group_live, one_group, (query_start, cache_start))
    rim_terms = jnp.concatenate([cache_acc[:, :REACH], cache_acc[:, REACH + blocks_here :]], axis=1)
    arrived = padded_2(rim_terms.astype(jnp.bfloat16), (("tp", 1),), REACH).astype(rim_terms.dtype)
    own_part = cache_acc[:, REACH : REACH + blocks_here]
    own_part = own_part.at[:, :REACH].add(arrived[:, :REACH])
    own_part = own_part.at[:, blocks_here - REACH :].add(arrived[:, 3 * REACH :])
    query_grad = query_acc.reshape(1, 1, heads_here, rows_here, HD).astype(jnp.bfloat16)
    cache_grad = own_part.reshape(1, 1, heads_here, rows_here, 2 * HD).astype(jnp.bfloat16)
    return (query_grad, cache_grad)


def solution(mesh):
    placed = (
        P("pipe", "tp", "seq", None),
        P("pipe", "tp", "seq", None),
        P("pipe", "tp", "seq", None),
        P("pipe", "tp", "seq", None, None),
        P("pipe", "tp", "seq", None),
        P(),
    )
    return jax.shard_map(
        body,
        mesh=mesh,
        in_specs=placed,
        out_specs=(P("pipe", "tp", "seq", None, None), P("pipe", "tp", "seq", None, None)),
        check_vma=False,
    )
```

profile of v0, /device:TPU:0, one launch (start us, length us, event | category | flops | bytes accessed | tf_op | source)
XLA Modules:
  0.0 304.5 jit_solution(2174274616329935110)
XLA Ops:
  0.6 1.3 copy.80
  1.9 2.5 collective-permute-start
  4.4 1.3 copy.79
  5.6 1.3 copy.81
  6.9 4.1 %collective-permute-done = bf16[1,1,96,2048]{2,3,1,0:T(8,128)(2,1)S(1)} collective-permute-done((bf16[1,1,96,2048]{2,3,1,0:T(8,128)(2,1)S(1)}, bf16[1,1,96,2048]{2,3,1,0:T(8,128)(2,1)S(1)}, u32[]{:S(2)}, u32[]{:S(2)}) %collective-permute-start) | collective-permute-done | bytes 393248 | tf_op jit(solution)/shard_map/ppermute | solution.py:19
  11.1 1.6 pad_maximum_fusion.1
  12.6 4.9 %all-to-all-start = ((bf16[96,32,192]{0,2,1:T(8,128)(2,1)}), bf16[96,32,192]{0,2,1:T(8,128)(2,1)S(1)}, u32[]{:S(2)}, u32[]{:S(2)}) async-start(bf16[96,32,192]{0,2,1:T(8,128)(2,1)} %pad_maximum_fusion.1), calls=%async_computation | async-start | bytes 3145728 | tf_op jit(solution)/shard_map/all_to_all | solution.py:53
  17.5 1.2 fusion.34
  18.7 3.4 %collective-permute-start.1 = (bf16[8,4,64,128]{3,2,1,0:T(8,128)(2,1)}, bf16[8,4,64,128]{3,2,1,0:T(8,128)(2,1)S(1)}, u32[]{:S(2)}, u32[]{:S(2)}) collective-permute-start(bf16[8,4,64,128]{3,2,1,0:T(8,128)(2,1)} %get-tuple-element.160), channel_id=1, source_target_pairs={{0,1},{2,3},{4,5},{6,7},{8,9},{10,11},{12,13},{14,15},{16,17},{18,... | collective-permute-start | bytes 1572872 | tf_op jit(solution)/shard_map/ppermute | solution.py:30
  22.1 1.3 collective-permute-start.2
  23.4 0.8 convert_reduce_fusion
  25.7 0.7 scatter_custom_fusion.3
  26.4 0.7 scatter_custom_fusion.2
  27.2 7.0 %collective-permute-done.1 = bf16[8,4,64,128]{3,2,1,0:T(8,128)(2,1)S(1)} collective-permute-done((bf16[8,4,64,128]{3,2,1,0:T(8,128)(2,1)}, bf16[8,4,64,128]{3,2,1,0:T(8,128)(2,1)S(1)}, u32[]{:S(2)}, u32[]{:S(2)}) %collective-permute-start.1) | collective-permute-done | bytes 524320 | tf_op jit(solution)/shard_map/ppermute | solution.py:30
  34.3 4.1 %collective-permute-done.2 = bf16[8,4,64,128]{3,2,1,0:T(8,128)(2,1)} collective-permute-done((bf16[8,4,64,128]{3,2,1,0:T(8,128)(2,1)}, bf16[8,4,64,128]{3,2,1,0:T(8,128)(2,1)}, u32[]{:S(2)}, u32[]{:S(2)}) %collective-permute-start.2) | collective-permute-done | bytes 524320 | tf_op jit(solution)/shard_map/ppermute | solution.py:32
  38.4 2.5 pad_maximum_fusion
  40.9 14.6 %all-to-all-done = bf16[96,32,192]{0,2,1:T(8,128)(2,1)S(1)} async-done(((bf16[96,32,192]{0,2,1:T(8,128)(2,1)}), bf16[96,32,192]{0,2,1:T(8,128)(2,1)S(1)}, u32[]{:S(2)}, u32[]{:S(2)}) %all-to-all-start) | async-done | bytes 1179680 | tf_op jit(solution)/shard_map/all_to_all | solution.py:53
  55.5 1.2 copy.109
  56.7 1.1 all_to_all.16
  59.0 2.3 broadcast_in_dim.15
  61.3 108.0 %while.14 = (s32[]{:T(128)}, f32[8,6,64,64]{3,2,1,0:T(8,128)S(1)}, f32[8,14,64,128]{3,2,1,0:T(8,128)}, s32[]{:T(128)}, s32[64]{0:T(128)S(1)}, /*index=5*/bf16[8,...) while((s32[]{:T(128)}, f32[8,6,64,64]{3,2,1,0:T(8,128)S(1)}, ...), condition=%wide.region_8.9_spmd, body=%wide.region_5.8_spmd.sunk | while | flops 688916736 | bytes 183445808 | solution.py:124
  63.3 0.7 copy.124
  64.0 4.5 %gather_fusion = bf16[32,8,64,128]{3,2,1,0:T(8,128)(2,1)} fusion(bf16[8,14,64,128]{3,2,1,0:T(8,128)(2,1)} %get-tuple-element.280, s32[1024]{0:T(1024)S(1)} %pad_clamp_fusion.4), kind=kCustom, calls=%fused_computation.1.clone.1 | custom fusion | bytes 8388736 | tf_op jit(solution)/shard_map/while/body/gather | solution.py:91
  68.5 5.5 %copy.123 = bf16[32,8,64,128]{3,2,0,1:T(8,128)(2,1)} copy(bf16[32,8,64,128]{3,2,1,0:T(8,128)(2,1)} %gather_fusion) | data formatting | bytes 8388608 | tf_op jit(solution)/shard_map/while/body/gather | solution.py:91
  74.0 3.0 gather_fusion.4
  77.0 3.1 %gather_fusion.1 = bf16[32,8,64,64]{3,2,1,0:T(8,128)(2,1)} fusion(bf16[8,6,64,64]{3,2,1,0:T(8,128)(2,1)S(1)} %get-tuple-element.278, s32[1024]{0:T(1024)S(1)} %pad_clamp_fusion.5), kind=kCustom, calls=%fused_computation.clone.1 | custom fusion | bytes 4194432 | tf_op jit(solution)/shard_map/while/body/gather | solution.py:87
  80.1 5.9 %fusion.71 = f32[8,32,64,64]{3,2,1,0:T(8,128)S(1)} fusion(bf16[8,32,64,128]{3,2,1,0:T(8,128)(2,1)} %bitcast.70, bf16[32,8,64,64]{3,2,1,0:T(8,128)(2,1)} %gather_fusion.1), kind=kOutput, calls=%fused_computation.24.clone.1 | convolution fusion | flops 134217728 | bytes 10485760 | tf_op jit(solution)/shard_map/while/body/hgqd,hgkd->hgqk/dot_general | solution.py:95
  86.0 8.3 %multiply_convert_fusion.2 = bf16[8,32,64,64]{3,2,1,0:T(8,128)(2,1)} fusion(f32[8,32,64,64]{3,2,1,0:T(8,128)S(1)} %fusion.71, f32[8,32,64]{2,1,0:T(8,128)S(1)} %copy-done.3, f32[32]{0:T(128)S(1)} %compare_convert_fusion.2, f32[8,32,64]{2,1,0:T(8,128)S(1)} %copy.125, bf16[8,32,64,128]{3,2,1,0:T(8,128)(2,1)S(1)} %bitcast.72, ...), kind=kOutput, calls=%fused_computation.11.clone.1 | convolution fusion | flops 140509184 | bytes 12714112 | tf_op jit(solution)/shard_map/while/body/hgqd,hgkd->hgqk/dot_general | solution.py:100
  94.3 8.8 %fusion.72 = f32[8,32,64,64]{3,2,1,0:T(8,128)} fusion(f32[8,32,64,64]{3,2,1,0:T(8,128)S(1)} %fusion.71, f32[32]{0:T(128)S(1)} %compare_convert_fusion.2, f32[8,32,64]{2,1,0:T(8,128)S(1)} %copy.125, bf16[32,8,64,64]{3,2,1,0:T(8,128)(2,1)} %gather_fusion.4), kind=kOutput, calls=%fused_computation.14.clone.1 | convolution fusion | flops 138412032 | bytes 10551424 | tf_op jit(solution)/shard_map/while/body/hgqk,hgqd->hgkd/dot_general | solution.py:114
  103.1 7.0 %broadcast_multiply_fusion.2 = f32[8,32,64,64]{3,2,1,0:T(8,128)} fusion(bf16[8,32,64,64]{3,2,1,0:T(8,128)(2,1)} %multiply_convert_fusion.2, bf16[32,8,64,64]{3,2,1,0:T(8,128)(2,1)S(1)} %copy-done.1), kind=kOutput, calls=%fused_computation.21.clone.1 | convolution fusion | flops 135266304 | bytes 8388608 | tf_op jit(solution)/shard_map/while/body/hgqk,hgqd->hgkd/dot_general | solution.py:109
  110.1 11.9 %maximum_bitcast_fusion.2 = f32[32,8,64,128]{3,2,0,1:T(8,128)} fusion(f32[8,32,64,64]{3,2,1,0:T(8,128)} %fusion.72, f32[8,32,64,64]{3,2,1,0:T(8,128)} %broadcast_multiply_fusion.2), kind=kLoop, calls=%fused_computation.9.clone.1 | loop fusion | flops 2097152 | bytes 16777216 | tf_op jit(solution)/shard_map/while/body/concatenate | solution.py:118
  122.0 8.3 %copy.127 = f32[32,8,64,128]{3,2,1,0:T(8,128)} copy(f32[32,8,64,128]{3,2,0,1:T(8,128)} %maximum_bitcast_fusion.2) | data formatting | bytes 16777216 | tf_op jit(solution)/shard_map/while/body/concatenate | solution.py:118
  130.3 18.4 %scatter_fusion.1 = f32[8,14,64,128]{3,2,1,0:T(8,128)} fusion(f32[8,14,64,128]{3,2,1,0:T(8,128)} %get-tuple-element.259, s32[32]{0:T(128)S(1)} %get-tuple-element.240, f32[32,8,64,128]{3,2,1,0:T(8,128)} %copy.127), kind=kCustom, calls=%fused_computation.6.clone.1 | custom fusion | flops 2097152 | bytes 25165952 | tf_op jit(solution)/shard_map/while/body/scatter-add | solution.py:118
  148.6 4.7 %multiply_bitcast_fusion.2 = f32[32,8,64,64]{3,2,0,1:T(8,128)S(1)} fusion(bf16[8,32,64,64]{3,2,1,0:T(8,128)(2,1)} %multiply_convert_fusion.2, bf16[8,32,64,128]{3,2,1,0:T(8,128)(2,1)} %bitcast.71), kind=kOutput, calls=%fused_computation.10.clone.1 | convolution fusion | flops 135266304 | bytes 10485760 | tf_op jit(solution)/shard_map/while/body/hgqk,hgkd->hgqd/dot_general | solution.py:105
  153.3 4.1 %copy.126 = f32[32,8,64,64]{3,2,1,0:T(8,128)} copy(f32[32,8,64,64]{3,2,0,1:T(8,128)S(1)} %multiply_bitcast_fusion.2) | data formatting | bytes 8388608 | tf_op jit(solution)/shard_map/while/body/mul | solution.py:105
  157.4 11.7 %scatter_fusion = f32[8,6,64,64]{3,2,1,0:T(8,128)S(1)} fusion(f32[8,6,64,64]{3,2,1,0:T(8,128)S(1)} %get-tuple-element.258, s32[32]{0:T(128)S(1)} %get-tuple-element.239, f32[32,8,64,64]{3,2,1,0:T(8,128)} %copy.126), kind=kCustom, calls=%fused_computation.5.clone.1 | custom fusion | flops 1048576 | bytes 12583040 | tf_op jit(solution)/shard_map/while/body/scatter-add | solution.py:117
  169.3 2.4 convert.6
  171.8 1.1 fusion.33
  172.9 112.2 %collective-permute-start.3 = (bf16[8,4,64,128]{3,2,1,0:T(8,128)(2,1)}, bf16[8,4,64,128]{3,2,1,0:T(8,128)(2,1)}, u32[]{:S(2)}, u32[]{:S(2)}) collective-permute-start(bf16[8,4,64,128]{3,2,1,0:T(8,128)(2,1)} %get-tuple-element.156), channel_id=1, source_target_pairs={{0,1},{2,3},{4,5},{6,7},{8,9},{10,11},{12,13},{14,15},{16,17},{18,... | collective-permute-start | bytes 1572872 | tf_op jit(solution)/shard_map/ppermute | solution.py:30
  285.1 1.3 collective-permute-start.4
  286.4 1.5 slice.104
  287.9 1.0 convert_element_type.69
  288.9 2.1 copy.93
  291.1 4.7 %collective-permute-done.3 = bf16[8,4,64,128]{3,2,1,0:T(8,128)(2,1)} collective-permute-done((bf16[8,4,64,128]{3,2,1,0:T(8,128)(2,1)}, bf16[8,4,64,128]{3,2,1,0:T(8,128)(2,1)}, u32[]{:S(2)}, u32[]{:S(2)}) %collective-permute-start.3) | collective-permute-done | bytes 524320 | tf_op jit(solution)/shard_map/ppermute | solution.py:30
  295.7 4.9 %collective-permute-done.4 = bf16[8,4,64,128]{3,2,1,0:T(8,128)(2,1)} collective-permute-done((bf16[8,4,64,128]{3,2,1,0:T(8,128)(2,1)}, bf16[8,4,64,128]{3,2,1,0:T(8,128)(2,1)}, u32[]{:S(2)}, u32[]{:S(2)}) %collective-permute-start.4) | collective-permute-done | bytes 524320 | tf_op jit(solution)/shard_map/ppermute | solution.py:32
  300.6 1.5 fusion.27
  302.1 1.3 fusion.26
  303.5 1.0 convert_element_type.72
  (39 shorter events, 4.1 us)
Async XLA Ops:
  1.9 15.6 %copy-start.2 = (bf16[1,1,8,384,128]{4,3,2,1,0:T(8,128)(2,1)S(1)}, bf16[1,1,8,384,128]{4,3,2,1,0:T(8,128)(2,1)}, u32[]{:S(2)}) copy-start(bf16[1,1,8,384,128]{4,3,2,1,0:T(8,128)(2,1)} %param.15) | copy-start | bytes 2359300
  1.9 9.2 %collective-permute-start = (bf16[1,1,96,2048]{2,3,1,0:T(8,128)(2,1)S(1)}, bf16[1,1,96,2048]{2,3,1,0:T(8,128)(2,1)S(1)}, u32[]{:S(2)}, u32[]{:S(2)}) collective-permute-start(bf16[1,1,96,2048]{2,3,1,0:T(8,128)(2,1)S(1)} %copy.80), channel_id=1, source_target_pairs={{0,24},{8,0},{16,8},{24,16},{1,25},{9,1},{17,9},{25,17},{2,26},{10... | collective-permute-start | bytes 1179656 | tf_op jit(solution)/shard_map/ppermute | solution.py:19
  11.1 12.3 %copy-start.5 = (s32[12,7]{0,1:T(8,128)S(1)}, s32[12,7]{0,1:T(8,128)}, u32[]{:S(2)}) copy-start(s32[12,7]{0,1:T(8,128)} %param.17) | copy-start | bytes 1012
  11.1 16.0 %copy-start.4 = (f32[1,1,8,384]{3,2,1,0:T(8,128)S(1)}, f32[1,1,8,384]{3,2,1,0:T(8,128)}, u32[]{:S(2)}) copy-start(f32[1,1,8,384]{3,2,1,0:T(8,128)} %param.16) | copy-start | bytes 36868
  12.6 42.8 %all-to-all-start = ((bf16[96,32,192]{0,2,1:T(8,128)(2,1)}), bf16[96,32,192]{0,2,1:T(8,128)(2,1)S(1)}, u32[]{:S(2)}, u32[]{:S(2)}) async-start(bf16[96,32,192]{0,2,1:T(8,128)(2,1)} %pad_maximum_fusion.1), calls=%async_computation | async-start | bytes 3145728 | tf_op jit(solution)/shard_map/all_to_all | solution.py:53
  18.7 15.6 %collective-permute-start.1 = (bf16[8,4,64,128]{3,2,1,0:T(8,128)(2,1)}, bf16[8,4,64,128]{3,2,1,0:T(8,128)(2,1)S(1)}, u32[]{:S(2)}, u32[]{:S(2)}) collective-permute-start(bf16[8,4,64,128]{3,2,1,0:T(8,128)(2,1)} %get-tuple-element.160), channel_id=1, source_target_pairs={{0,1},{2,3},{4,5},{6,7},{8,9},{10,11},{12,13},{14,15},{16,17},{18,... | collective-permute-start | bytes 1572872 | tf_op jit(solution)/shard_map/ppermute | solution.py:30
  22.1 16.3 %collective-permute-start.2 = (bf16[8,4,64,128]{3,2,1,0:T(8,128)(2,1)}, bf16[8,4,64,128]{3,2,1,0:T(8,128)(2,1)}, u32[]{:S(2)}, u32[]{:S(2)}) collective-permute-start(bf16[8,4,64,128]{3,2,1,0:T(8,128)(2,1)} %get-tuple-element.161), channel_id=1, source_target_pairs={{1,0},{3,2},{5,4},{7,6},{9,8},{11,10},{13,12},{15,14},{17,16},{19,... | collective-permute-start | bytes 1572872 | tf_op jit(solution)/shard_map/ppermute | solution.py:32
  80.1 5.9 %copy-start = (bf16[32,8,64,128]{3,2,0,1:T(8,128)(2,1)S(1)}, bf16[32,8,64,128]{3,2,0,1:T(8,128)(2,1)}, u32[]{:S(2)}) copy-start(bf16[32,8,64,128]{3,2,0,1:T(8,128)(2,1)} %copy.123) | copy-start | bytes 12582916 | tf_op jit(solution)/shard_map/while
  80.1 5.9 %copy-start.3 = (f32[8,32,64]{2,1,0:T(8,128)S(1)}, f32[8,32,64]{2,1,0:T(8,128)}, u32[]{:S(2)}) copy-start(f32[8,32,64]{2,1,0:T(8,128)} %copy.124) | copy-start | bytes 196612 | tf_op jit(solution)/shard_map/while
  94.3 8.8 %copy-start.1 = (bf16[32,8,64,64]{3,2,1,0:T(8,128)(2,1)S(1)}, bf16[32,8,64,64]{3,2,1,0:T(8,128)(2,1)}, u32[]{:S(2)}) copy-start(bf16[32,8,64,64]{3,2,1,0:T(8,128)(2,1)} %gather_fusion.1) | copy-start | bytes 6291460 | tf_op jit(solution)/shard_map/while
  172.9 122.8 %collective-permute-start.3 = (bf16[8,4,64,128]{3,2,1,0:T(8,128)(2,1)}, bf16[8,4,64,128]{3,2,1,0:T(8,128)(2,1)}, u32[]{:S(2)}, u32[]{:S(2)}) collective-permute-start(bf16[8,4,64,128]{3,2,1,0:T(8,128)(2,1)} %get-tuple-element.156), channel_id=1, source_target_pairs={{0,1},{2,3},{4,5},{6,7},{8,9},{10,11},{12,13},{14,15},{16,17},{18,... | collective-permute-start | bytes 1572872 | tf_op jit(solution)/shard_map/ppermute | solution.py:30
  285.1 15.5 %collective-permute-start.4 = (bf16[8,4,64,128]{3,2,1,0:T(8,128)(2,1)}, bf16[8,4,64,128]{3,2,1,0:T(8,128)(2,1)}, u32[]{:S(2)}, u32[]{:S(2)}) collective-permute-start(bf16[8,4,64,128]{3,2,1,0:T(8,128)(2,1)} %get-tuple-element.157), channel_id=1, source_target_pairs={{1,0},{3,2},{5,4},{7,6},{9,8},{11,10},{13,12},{15,14},{17,16},{19,... | collective-permute-start | bytes 1572872 | tf_op jit(solution)/shard_map/ppermute | solution.py:32
where the time goes:
time: 305 us; the launch traced here: 304 us
  starting transfers between devices  126 us (41%)
  other arithmetic  55.1 us (18%)
  local copies, waits for them, and re-layouts  47.9 us (16%)
  waiting for transfers between devices  39.5 us (13%)
  matrix products  34.7 us (11%)
    ppermute x2, starting transfers between devices, padded_2(): lax.ppermute(tail, axis, [(i, (i + 1) % count) for i in range(ends)])  116 us
    scatter-add x1, other arithmetic, one_group(): cache_acc.at[:, key_pick]  18.4 us
    all_to_all x1, waiting for transfers between devices, body(): lax.all_to_all(packed, 'seq', split_axis=1, concat_axis=0, tiled=True)  14.6 us
    concatenate x1, other arithmetic, one_group(): jnp.concatenate([key_part, value_part], axis=-1)  11.9 us
    scatter-add x1, other arithmetic, one_group(): query_acc = query_acc.at[:, query_pick].add(query_part)  11.7 us
    ppermute x2, waiting for transfers between devices, padded_2(): lax.ppermute(tail, axis, [(i, (i + 1) % count) for i in range(ends)])  11.7 us
    gather x2, local copies, waits for them, and re-layouts, one_group(): cache_rows = padded[:, key_pick]  10 us
    ppermute x2, waiting for transfers between devices, padded_2(): lax.ppermute(head, axis, [((i + 1) % count, i) for i in range(ends)])  9.06 us
  transfers between devices with their start and end apart: 6, of which 6 were waited for; matrix products, arithmetic and copies ran while one was open for 5% of the time, Pallas kernels for 0%

commit v1 on v0

--- a/solution.py
+++ b/solution.py
@@ -1,6 +1,8 @@
 import jax
 import jax.numpy as jnp
 from jax import lax
+from jax.experimental import pallas as pl
+from jax.experimental.pallas import tpu as pltpu
 from jax.sharding import PartitionSpec as P
 
 H = 32
@@ -42,7 +44,7 @@
     return turned.reshape(heads_here, blocks_here, BLK, values.shape[2])
 
 
-def body(upstream, queries, attention_out, keys_values, log_totals, neighbours):
+def general_body(upstream, queries, attention_out, keys_values, log_totals, neighbours):
     tokens_here = queries.shape[2]
     inv_root = HD ** (-0.5)
     incoming = passed_along(upstream, "pipe", -1)
@@ -132,6 +134,342 @@
     return (query_grad, cache_grad)
 
 
+MESH = pl.DeviceIdType.MESH
+LANES = 128
+PER_TILE = LANES // HD
+LOG2E = 1.4426950408889634
+ABSENT = -1e30
+NT = (((1,), (1,)), ((), ()))
+TN = (((0,), (0,)), ((), ()))
+
+
+def dot_f32(left, right, dims=(((1,), (0,)), ((), ()))):
+    return lax.dot_general(left, right, dims, preferred_element_type=jnp.float32)
+
+
+def listed_bias(neigh_ref, first_row, first_key, key_rows, blocks_here):
+    lane = lax.broadcasted_iota(jnp.int32, (key_rows, LANES), 1)
+    key = lax.broadcasted_iota(jnp.int32, (key_rows, LANES), 0) + first_key
+    tiles = []
+    for pair in range(blocks_here // 2):
+        found = None
+        for slot in range(NBR):
+            here = jnp.where(
+                lane < BLK,
+                neigh_ref[slot, first_row + 2 * pair],
+                neigh_ref[slot, first_row + 2 * pair + 1],
+            )
+            hit = (key == here).astype(jnp.float32)
+            found = hit if found is None else jnp.maximum(found, hit)
+        tiles.append((found - 1.0) * -ABSENT)
+    return jnp.concatenate(tiles, axis=1)
+
+
+def fused_kernel(
+    neigh_ref, norm_ref, up_ref, query_ref, out_ref, cache_ref, dq_ref, dkv_ref,
+    inc, outs, kv, halo, qbuf, gbuf, dsend, dgot, acc, acc_kv, back_out, back_in, bias_own, bias_halo, rows_aux,
+    up_send, up_recv, q_send, q_recv, g_send, g_recv, d_send, d_recv, h_send, h_recv, b_send, b_recv, local_sem,
+):
+    n_pipe, n_seq = lax.axis_size("pipe"), lax.axis_size("seq")
+    pipe, seq, tp = lax.axis_index("pipe"), lax.axis_index("seq"), lax.axis_index("tp")
+    tokens, width = inc.shape
+    heads, rows, _ = kv.shape
+    tiles = heads // PER_TILE
+    span = REACH * BLK
+    blocks_here = rows // BLK
+    share = heads * HD
+    below, above = lax.rem(pipe + n_pipe - 1, n_pipe), lax.rem(pipe + 1, n_pipe)
+    mate = 1 - tp
+    window = pl.multiple_of(mate * (rows - span), LANES)
+    mine = pl.multiple_of(seq * tokens, 16)
+
+    def peer(step):
+        return lax.rem(seq + step, n_seq)
+
+    def tile_cols(dest, tile):
+        return pl.ds(pl.multiple_of(dest * share + tile * LANES, LANES), LANES)
+
+    def up_copy(tile, dest):
+        cols = pl.ds(dest * share + tile * LANES, LANES)
+        return pltpu.make_async_remote_copy(
+            src_ref=up_ref.at[:, cols], dst_ref=inc.at[:, cols],
+            send_sem=up_send.at[tile, dest], recv_sem=up_recv.at[tile, dest],
+            device_id={"pipe": below}, device_id_type=MESH,
+        )
+
+    def q_copy(tile, step):
+        return pltpu.make_async_remote_copy(
+            src_ref=query_ref.at[:, tile_cols(peer(step), tile)],
+            dst_ref=qbuf.at[tile, pl.ds(mine, tokens), :],
+            send_sem=q_send.at[tile, step - 1], recv_sem=q_recv.at[tile, step - 1],
+            device_id={"seq": peer(step)}, device_id_type=MESH,
+        )
+
+    def g_copy(tile, step):
+        return pltpu.make_async_remote_copy(
+            src_ref=inc.at[:, tile_cols(peer(step), tile)],
+            dst_ref=gbuf.at[tile, pl.ds(mine, tokens), :],
+            send_sem=g_send.at[tile, step - 1], recv_sem=g_recv.at[tile, step - 1],
+            device_id={"seq": peer(step)}, device_id_type=MESH,
+        )
+
+    def d_copy(step):
+        return pltpu.make_async_remote_copy(
+            src_ref=dsend.at[peer(step)], dst_ref=dgot.at[seq],
+            send_sem=d_send.at[step - 1], recv_sem=d_recv.at[step - 1],
+            device_id={"seq": peer(step)}, device_id_type=MESH,
+        )
+
+    def h_copy(tile):
+        pair = pl.ds(tile * PER_TILE, PER_TILE)
+        return pltpu.make_async_remote_copy(
+            src_ref=cache_ref.at[pair, pl.ds(window, span), :], dst_ref=halo.at[pair],
+            send_sem=h_send.at[tile], recv_sem=h_recv.at[tile],
+            device_id={"tp": mate}, device_id_type=MESH,
+        )
+
+    def b_copy(tile):
+        pair = pl.ds(tile * PER_TILE, PER_TILE)
+        return pltpu.make_async_remote_copy(
+            src_ref=back_out.at[pair], dst_ref=back_in.at[pair],
+            send_sem=b_send.at[tile], recv_sem=b_recv.at[tile],
+            device_id={"tp": mate}, device_id_type=MESH,
+        )
+
+    out_local = pltpu.make_async_copy(out_ref, outs, local_sem.at[0])
+    kv_local = pltpu.make_async_copy(cache_ref, kv, local_sem.at[1])
+    q_local = [
+        pltpu.make_async_copy(
+            query_ref.at[:, tile_cols(seq, tile)], qbuf.at[tile, pl.ds(mine, tokens), :], local_sem.at[2 + tile]
+        )
+        for tile in range(tiles)
+    ]
+    out_local.start()
+    kv_local.start()
+    for copy in q_local:
+        copy.start()
+
+    barrier = pltpu.get_barrier_semaphore()
+    pl.semaphore_signal(barrier, inc=1, device_id={"pipe": above}, device_id_type=MESH)
+    pl.semaphore_signal(barrier, inc=1, device_id={"tp": mate}, device_id_type=MESH)
+    for step in range(1, n_seq):
+        pl.semaphore_signal(barrier, inc=1, device_id={"seq": peer(step)}, device_id_type=MESH)
+    pl.semaphore_wait(barrier, n_seq + 1)
+
+    for tile in range(tiles):
+        for dest in range(n_seq):
+            up_copy(tile, dest).start()
+        h_copy(tile).start()
+        if tile < 2:
+            for step in range(1, n_seq):
+                q_copy(tile, step).start()
+
+    first_row = tp * blocks_here
+    halo_key = mate * blocks_here + tp * (blocks_here - REACH)
+    bias_own[...] = listed_bias(neigh_ref, first_row, first_row, bias_own.shape[0], blocks_here)
+    bias_halo[...] = listed_bias(neigh_ref, first_row, halo_key, bias_halo.shape[0], blocks_here)
+
+    for tile in range(tiles):
+        for dest in range(n_seq):
+            up_copy(tile, dest).wait_recv()
+        for step in range(1, n_seq):
+            g_copy(tile, step).start()
+        if tile + 2 < tiles:
+            for step in range(1, n_seq):
+                q_copy(tile + 2, step).start()
+
+    out_local.wait()
+    picks = (
+        lax.broadcasted_iota(jnp.int32, (heads, share), 1) // HD
+        == lax.broadcasted_iota(jnp.int32, (heads, share), 0)
+    ).astype(jnp.bfloat16)
+    dsend[...] = jnp.zeros_like(dsend)
+    for dest in range(n_seq):
+        cols = pl.ds(dest * share, share)
+        terms = inc[:, cols].astype(jnp.float32) * outs[:, cols].astype(jnp.float32)
+        high = terms.astype(jnp.bfloat16)
+        low = (terms - high.astype(jnp.float32)).astype(jnp.bfloat16)
+        dsend[dest, :, :tokens] = dot_f32(picks, high, NT) + dot_f32(picks, low, NT)
+    for step in range(1, n_seq):
+        d_copy(step).start()
+    dgot[seq] = dsend[seq]
+    for tile in range(tiles):
+        gbuf[tile, pl.ds(mine, tokens), :] = inc[:, tile_cols(seq, tile)]
+    kv_local.wait()
+    for copy in q_local:
+        copy.wait()
+    for step in range(1, n_seq):
+        d_copy(step).wait_recv()
+    delta = None
+    for source in range(n_seq):
+        part = jnp.concatenate([dgot[source], jnp.zeros((heads, rows - LANES), jnp.float32)], axis=1)
+        if source:
+            part = pltpu.roll(part, source * tokens, 1)
+        delta = part if delta is None else delta + part
+    norm = norm_ref[...] * LOG2E
+    for head in range(heads):
+        rows_aux[head, 0:1, :] = norm[head : head + 1]
+        rows_aux[head, 1:2, :] = delta[head : head + 1]
+
+    inv_root = HD ** (-0.5)
+
+    def block_terms(keys, values, q_rows, g_rows, bias, norm_row, delta_row):
+        count = keys.shape[0] // BLK
+        scores = dot_f32(keys, q_rows, NT) * (inv_root * LOG2E)
+        shift = bias[:count] - norm_row
+        scores = scores.reshape(count, BLK, scores.shape[1]) + shift[:, None, :]
+        weights = jnp.exp2(scores).reshape(keys.shape[0], scores.shape[2])
+        grad_weights = dot_f32(values, g_rows, NT)
+        grad_scores = (weights * (grad_weights - delta_row)).astype(jnp.bfloat16)
+        key_part = dot_f32(grad_scores, q_rows) * inv_root
+        value_part = dot_f32(weights.astype(jnp.bfloat16), g_rows)
+        query_part = dot_f32(keys, grad_scores, TN) * inv_root
+        return query_part, jnp.concatenate([key_part, value_part], axis=1)
+
+    def one_tile(tile, carry):
+        for step in range(1, n_seq):
+            q_copy(tile, step).wait_recv()
+            g_copy(tile, step).wait_recv()
+        h_copy(tile).wait_recv()
+        for inner in range(PER_TILE):
+            head = tile * PER_TILE + inner
+            lanes = slice(inner * HD, (inner + 1) * HD)
+            query_part, cache_part = block_terms(
+                halo[head, :, :HD],
+                halo[head, :, HD:],
+                qbuf[tile, pl.ds(window, span), lanes],
+                gbuf[tile, pl.ds(window, span), lanes],
+                bias_halo[:, pl.ds(window, span)],
+                rows_aux[head, 0:1, pl.ds(window, span)],
+                rows_aux[head, 1:2, pl.ds(window, span)],
+            )
+            back_out[head] = cache_part.astype(jnp.bfloat16)
+            acc[head, :, pl.ds(window, span)] = query_part
+            acc[head, :, pl.ds(pl.multiple_of(tp * span, LANES), rows - span)] = jnp.zeros(
+                (HD, rows - span), jnp.float32
+            )
+        b_copy(tile).start()
+        for inner in range(PER_TILE):
+            head = tile * PER_TILE + inner
+            lanes = slice(inner * HD, (inner + 1) * HD)
+            query_part, cache_part = block_terms(
+                kv[head, :, :HD],
+                kv[head, :, HD:],
+                qbuf[tile, :, lanes],
+                gbuf[tile, :, lanes],
+                bias_own[...],
+                rows_aux[head, 0:1, :],
+                rows_aux[head, 1:2, :],
+            )
+            dq_ref[head] = (acc[head] + query_part).astype(jnp.bfloat16)
+            acc_kv[head] = cache_part
+        return carry
+
+    lax.fori_loop(0, tiles, one_tile, 0)
+
+    def finish(tile, carry):
+        b_copy(tile).wait_recv()
+        for inner in range(PER_TILE):
+            head = tile * PER_TILE + inner
+            acc_kv[head, pl.ds(window, span), :] += back_in[head].astype(jnp.float32)
+            dkv_ref[head] = acc_kv[head].astype(jnp.bfloat16)
+        return carry
+
+    lax.fori_loop(0, tiles, finish, 0)
+
+    for tile in range(tiles):
+        for dest in range(n_seq):
+            up_copy(tile, dest).wait_send()
+        for step in range(1, n_seq):
+            q_copy(tile, step).wait_send()
+            g_copy(tile, step).wait_send()
+        h_copy(tile).wait_send()
+        b_copy(tile).wait_send()
+    for step in range(1, n_seq):
+        d_copy(step).wait_send()
+
+
+def fused_body(upstream, queries, attention_out, keys_values, log_totals, neighbours):
+    tokens, width = queries.shape[2:]
+    heads, rows = keys_values.shape[2:4]
+    tiles = heads // PER_TILE
+    n_seq = lax.axis_size("seq")
+    span = REACH * BLK
+    blocks_pad = 8 * -(-(rows // BLK) // 8)
+    bf16, f32 = jnp.bfloat16, jnp.float32
+    vmem = pl.BlockSpec(memory_space=pltpu.VMEM)
+    anywhere = pl.BlockSpec(memory_space=pl.ANY)
+    dma = pltpu.SemaphoreType.DMA
+    query_turned, cache_grad = pl.pallas_call(
+        fused_kernel,
+        out_shape=(
+            jax.ShapeDtypeStruct((heads, HD, rows), bf16),
+            jax.ShapeDtypeStruct((heads, rows, 2 * HD), bf16),
+        ),
+        in_specs=[pl.BlockSpec(memory_space=pltpu.SMEM), vmem] + [anywhere] * 4,
+        out_specs=(vmem, vmem),
+        scratch_shapes=[
+            pltpu.VMEM((tokens, width), bf16),
+            pltpu.VMEM((tokens, width), bf16),
+            pltpu.VMEM((heads, rows, 2 * HD), bf16),
+            pltpu.VMEM((heads, span, 2 * HD), bf16),
+            pltpu.VMEM((tiles, rows, LANES), bf16),
+            pltpu.VMEM((tiles, rows, LANES), bf16),
+            pltpu.VMEM((n_seq, heads, LANES), f32),
+            pltpu.VMEM((n_seq, heads, LANES), f32),
+            pltpu.VMEM((heads, HD, rows), f32),
+            pltpu.VMEM((heads, rows, 2 * HD), f32),
+            pltpu.VMEM((heads, span, 2 * HD), bf16),
+            pltpu.VMEM((heads, span, 2 * HD), bf16),
+            pltpu.VMEM((blocks_pad, rows), f32),
+            pltpu.VMEM((8, rows), f32),
+            pltpu.VMEM((heads, 8, rows), f32),
+            dma((tiles, n_seq)),
+            dma((tiles, n_seq)),
+            dma((tiles, n_seq - 1)),
+            dma((tiles, n_seq - 1)),
+            dma((tiles, n_seq - 1)),
+            dma((tiles, n_seq - 1)),
+            dma((n_seq - 1,)),
+            dma((n_seq - 1,)),
+            dma((tiles,)),
+            dma((tiles,)),
+            dma((tiles,)),
+            dma((tiles,)),
+            dma((2 + tiles,)),
+        ],
+        compiler_params=pltpu.CompilerParams(
+            collective_id=0, has_side_effects=True, vmem_limit_bytes=48 * 1024 * 1024
+        ),
+    )(
+        jnp.transpose(neighbours),
+        log_totals.reshape(heads, rows),
+        upstream.reshape(tokens, width),
+        queries.reshape(tokens, width),
+        attention_out.reshape(tokens, width),
+        keys_values.reshape(heads, rows, 2 * HD),
+    )
+    query_grad = jnp.transpose(query_turned, (0, 2, 1)).reshape(1, 1, heads, rows, HD)
+    return query_grad, cache_grad.reshape(1, 1, heads, rows, 2 * HD)
+
+
+def body(upstream, queries, attention_out, keys_values, log_totals, neighbours):
+    tokens = queries.shape[2]
+    heads, rows = keys_values.shape[2:4]
+    fits = (
+        lax.axis_size("tp") == 2
+        and lax.axis_size("pipe") > 1
+        and lax.axis_size("seq") > 1
+        and heads == 8
+        and tokens % 16 == 0
+        and tokens <= LANES
+        and rows % LANES == 0
+        and REACH * BLK < rows <= 512
+    )
+    chosen = fused_body if fits else general_body
+    return chosen(upstream, queries, attention_out, keys_values, log_totals, neighbours)
+
+
 def solution(mesh):
     placed = (
         P("pipe", "tp", "seq", None),

time: 305 us -> 47.3 us (0.16)
  starting transfers between devices: 126 us -> 0 us
  other arithmetic: 55.1 us -> 0 us
  local copies, waits for them, and re-layouts: 47.9 us -> 7.13 us
  waiting for transfers between devices: 39.5 us -> 0 us
  Pallas kernels: 0 us -> 39.2 us
  matrix products: 34.7 us -> 0 us
    ppermute x5 -> x0, starting transfers between devices: 121 us -> none  [the longest x2 116 us: padded_2(): lax.ppermute(tail, axis, [(i, (i + 1) % count) for i in range(ends)])]
    pallas_call x0 -> x1, Pallas kernels: none -> 39.2 us  [fused_body(): pl.pallas_call(fused_kernel, out_shape=(jax.ShapeDtypeStruct((heads, HD,...]
    dot_general x5 -> x0, matrix products: 34.7 us -> none  [the longest x1 8.77 us: one_group(): jnp.einsum('hgqk,hgqd->hgkd', weights_half, grad_rows, preferred_element_...]
    scatter-add x4 -> x0, other arithmetic: 32.9 us -> none  [the longest x1 18.4 us: one_group(): cache_acc.at[:, key_pick]]
    ppermute x5 -> x0, waiting for transfers between devices: 24.9 us -> none  [the longest x2 11.7 us: padded_2(): lax.ppermute(tail, axis, [(i, (i + 1) % count) for i in range(ends)])]
    gather x8 -> x0, local copies, waits for them, and re-layouts: 18 us -> none  [the longest x2 10 us: one_group(): cache_rows = padded[:, key_pick]]
    concatenate x3 -> x0, other arithmetic: 15.9 us -> none  [the longest x1 11.9 us: one_group(): jnp.concatenate([key_part, value_part], axis=-1)]
    all_to_all x1 -> x0, waiting for transfers between devices: 14.6 us -> none  [body(): lax.all_to_all(packed, 'seq', split_axis=1, concat_axis=0, tiled=True)]
  transfers between devices with their start and end apart: 6 -> 0, of which waited for: 6 -> 0; matrix products, arithmetic and copies ran while one was open for 5% -> 0% of each run, Pallas kernels for 0% -> 0%
where the time goes in v1:
time: 47.3 us; the launch traced here: 47 us
  Pallas kernels  39.2 us (83%)
  local copies, waits for them, and re-layouts  7.13 us (15%)
  between operations  0.65 us (1%)
    pallas_call x1, Pallas kernels, fused_body(): pl.pallas_call(fused_kernel, out_shape=(jax.ShapeDtypeStruct((heads, HD,...  39.2 us
    unnamed x14, local copies, waits for them, and re-layouts  7.13 us

profile of v1, /device:TPU:0, one launch (start us, length us, event | category | flops | bytes accessed | tf_op | source)
XLA Modules:
  0.0 47.0 jit_solution(10146684933220412602)
XLA Ops:
  0.6 0.0 copy-start.5
  0.6 0.7 %copy-done.5 = s32[12,7]{0,1:T(8,128)S(1)} copy-done((s32[12,7]{0,1:T(8,128)S(1)}, s32[12,7]{0,1:T(8,128)}, u32[]{:S(2)}) %copy-start.5) | copy-done | bytes 360
  1.3 0.0 copy-start
  1.3 1.1 %copy-done = bf16[1,1,8,384,128]{4,3,2,1,0:T(8,128)(2,1)S(1)} copy-done((bf16[1,1,8,384,128]{4,3,2,1,0:T(8,128)(2,1)S(1)}, bf16[1,1,8,384,128]{4,3,2,1,0:T(8,128)(2,1)}, u32[]{:S(2)}) %copy-start) | copy-done | bytes 786456
  2.5 0.0 copy-start.1
  2.5 1.0 %copy-done.1 = bf16[1,1,96,2048]{3,2,1,0:T(8,128)(2,1)S(1)} copy-done((bf16[1,1,96,2048]{3,2,1,0:T(8,128)(2,1)S(1)}, bf16[1,1,96,2048]{3,2,1,0:T(8,128)(2,1)}, u32[]{:S(2)}) %copy-start.1) | copy-done | bytes 393240
  3.4 0.0 copy-start.2
  3.5 1.0 %copy-done.2 = bf16[1,1,96,2048]{3,2,1,0:T(8,128)(2,1)S(1)} copy-done((bf16[1,1,96,2048]{3,2,1,0:T(8,128)(2,1)S(1)}, bf16[1,1,96,2048]{3,2,1,0:T(8,128)(2,1)}, u32[]{:S(2)}) %copy-start.2) | copy-done | bytes 393240
  4.4 0.0 copy-start.3
  4.4 1.0 %copy-done.3 = bf16[1,1,96,2048]{3,2,1,0:T(8,128)(2,1)S(1)} copy-done((bf16[1,1,96,2048]{3,2,1,0:T(8,128)(2,1)S(1)}, bf16[1,1,96,2048]{3,2,1,0:T(8,128)(2,1)}, u32[]{:S(2)}) %copy-start.3) | copy-done | bytes 393240
  5.4 0.0 copy-start.4
  5.4 0.7 %copy-done.4 = f32[1,1,8,384]{3,2,1,0:T(8,128)S(1)} copy-done((f32[1,1,8,384]{3,2,1,0:T(8,128)S(1)}, f32[1,1,8,384]{3,2,1,0:T(8,128)}, u32[]{:S(2)}) %copy-start.4) | copy-done | bytes 12312
  6.1 39.2 %shard_map.77 = (bf16[8,64,384]{2,1,0:T(8,128)(2,1)S(1)}, bf16[8,384,128]{2,1,0:T(8,128)(2,1)S(1)}) custom-call(s32[7,12]{1,0:T(8,128)S(1)} %bitcast.17, f32[8,384]{1,0:T(8,128)S(1)} %bitcast.16, bf16[96,2048]{1,0:T(8,128)(2,1)S(1)} %bitcast.13, bf16[96,2048]{1,0:T(8,128)(2,1)S(1)} %bitcast.14, bf16[96,2048]{1,0:T(8,128)(2,1)S(1)} %bitcast.15, ...), custom_call_target="tpu_custom_call" | custom-call | tf_op jit(solution)/shard_map/pallas_call | solution.py:403
  45.4 0.7 %copy.10 = bf16[1,1,8,384,64]{3,4,2,1,0:T(8,128)(2,1)} copy(bf16[1,1,8,384,64]{3,4,2,1,0:T(8,128)(2,1)S(1)} %bitcast.12) | data formatting | bytes 786432
  46.1 0.9 %copy.11 = bf16[1,1,8,384,128]{4,3,2,1,0:T(8,128)(2,1)} copy(bf16[1,1,8,384,128]{4,3,2,1,0:T(8,128)(2,1)S(1)} %bitcast.10) | data formatting | bytes 1572864
Async XLA Ops:
  0.6 0.7 %copy-start.5 = (s32[12,7]{0,1:T(8,128)S(1)}, s32[12,7]{0,1:T(8,128)}, u32[]{:S(2)}) copy-start(s32[12,7]{0,1:T(8,128)} %param.11) | copy-start | bytes 1012
  1.3 1.1 %copy-start = (bf16[1,1,8,384,128]{4,3,2,1,0:T(8,128)(2,1)S(1)}, bf16[1,1,8,384,128]{4,3,2,1,0:T(8,128)(2,1)}, u32[]{:S(2)}) copy-start(bf16[1,1,8,384,128]{4,3,2,1,0:T(8,128)(2,1)} %param.9) | copy-start | bytes 2359300
  2.5 1.0 %copy-start.1 = (bf16[1,1,96,2048]{3,2,1,0:T(8,128)(2,1)S(1)}, bf16[1,1,96,2048]{3,2,1,0:T(8,128)(2,1)}, u32[]{:S(2)}) copy-start(bf16[1,1,96,2048]{3,2,1,0:T(8,128)(2,1)} %param.6) | copy-start | bytes 1179652
  3.4 1.0 %copy-start.2 = (bf16[1,1,96,2048]{3,2,1,0:T(8,128)(2,1)S(1)}, bf16[1,1,96,2048]{3,2,1,0:T(8,128)(2,1)}, u32[]{:S(2)}) copy-start(bf16[1,1,96,2048]{3,2,1,0:T(8,128)(2,1)} %param.7) | copy-start | bytes 1179652
  4.4 1.0 %copy-start.3 = (bf16[1,1,96,2048]{3,2,1,0:T(8,128)(2,1)S(1)}, bf16[1,1,96,2048]{3,2,1,0:T(8,128)(2,1)}, u32[]{:S(2)}) copy-start(bf16[1,1,96,2048]{3,2,1,0:T(8,128)(2,1)} %param.8) | copy-start | bytes 1179652
  5.4 0.7 %copy-start.4 = (f32[1,1,8,384]{3,2,1,0:T(8,128)S(1)}, f32[1,1,8,384]{3,2,1,0:T(8,128)}, u32[]{:S(2)}) copy-start(f32[1,1,8,384]{3,2,1,0:T(8,128)} %param.10) | copy-start | bytes 36868

commit v2 on v1

--- a/solution.py
+++ b/solution.py
@@ -137,7 +137,6 @@
 MESH = pl.DeviceIdType.MESH
 LANES = 128
 PER_TILE = LANES // HD
-LOG2E = 1.4426950408889634
 ABSENT = -1e30
 NT = (((1,), (1,)), ((), ()))
 TN = (((0,), (0,)), ((), ()))
@@ -166,8 +165,8 @@
 
 
 def fused_kernel(
-    neigh_ref, norm_ref, up_ref, query_ref, out_ref, cache_ref, dq_ref, dkv_ref,
-    inc, outs, kv, halo, qbuf, gbuf, dsend, dgot, acc, acc_kv, back_out, back_in, bias_own, bias_halo, rows_aux,
+    neigh_hbm, norm_hbm, up_ref, query_ref, out_ref, cache_ref, dq_ref, dkv_ref,
+    neigh_ref, norm_ref, inc, outs, kv, halo, qbuf, gbuf, dsend, dgot, acc, acc_kv, back_out, back_in, bias_own, bias_halo, rows_aux,
     up_send, up_recv, q_send, q_recv, g_send, g_recv, d_send, d_recv, h_send, h_recv, b_send, b_recv, local_sem,
 ):
     n_pipe, n_seq = lax.axis_size("pipe"), lax.axis_size("seq")
@@ -244,6 +243,10 @@
         )
         for tile in range(tiles)
     ]
+    neigh_local = pltpu.make_async_copy(neigh_hbm, neigh_ref, local_sem.at[2 + tiles])
+    norm_local = pltpu.make_async_copy(norm_hbm, norm_ref, local_sem.at[3 + tiles])
+    neigh_local.start()
+    norm_local.start()
     out_local.start()
     kv_local.start()
     for copy in q_local:
@@ -264,6 +267,7 @@
             for step in range(1, n_seq):
                 q_copy(tile, step).start()
 
+    neigh_local.wait()
     first_row = tp * blocks_here
     halo_key = mate * blocks_here + tp * (blocks_here - REACH)
     bias_own[...] = listed_bias(neigh_ref, first_row, first_row, bias_own.shape[0], blocks_here)
@@ -306,7 +310,8 @@
         if source:
             part = pltpu.roll(part, source * tokens, 1)
         delta = part if delta is None else delta + part
-    norm = norm_ref[...] * LOG2E
+    norm_local.wait()
+    norm = norm_ref[...]
     for head in range(heads):
         rows_aux[head, 0:1, :] = norm[head : head + 1]
         rows_aux[head, 1:2, :] = delta[head : head + 1]
@@ -315,15 +320,16 @@
 
     def block_terms(keys, values, q_rows, g_rows, bias, norm_row, delta_row):
         count = keys.shape[0] // BLK
-        scores = dot_f32(keys, q_rows, NT) * (inv_root * LOG2E)
+        keys = keys * jnp.bfloat16(inv_root)
+        scores = dot_f32(keys, q_rows, NT)
         shift = bias[:count] - norm_row
         scores = scores.reshape(count, BLK, scores.shape[1]) + shift[:, None, :]
-        weights = jnp.exp2(scores).reshape(keys.shape[0], scores.shape[2])
+        weights = jnp.exp(scores).reshape(keys.shape[0], scores.shape[2])
         grad_weights = dot_f32(values, g_rows, NT)
         grad_scores = (weights * (grad_weights - delta_row)).astype(jnp.bfloat16)
         key_part = dot_f32(grad_scores, q_rows) * inv_root
         value_part = dot_f32(weights.astype(jnp.bfloat16), g_rows)
-        query_part = dot_f32(keys, grad_scores, TN) * inv_root
+        query_part = dot_f32(keys, grad_scores, TN)
         return query_part, jnp.concatenate([key_part, value_part], axis=1)
 
     def one_tile(tile, carry):
@@ -398,7 +404,7 @@
     blocks_pad = 8 * -(-(rows // BLK) // 8)
     bf16, f32 = jnp.bfloat16, jnp.float32
     vmem = pl.BlockSpec(memory_space=pltpu.VMEM)
-    anywhere = pl.BlockSpec(memory_space=pl.ANY)
+    pinned = pl.BlockSpec(memory_space=pltpu.HBM)
     dma = pltpu.SemaphoreType.DMA
     query_turned, cache_grad = pl.pallas_call(
         fused_kernel,
@@ -406,9 +412,11 @@
             jax.ShapeDtypeStruct((heads, HD, rows), bf16),
             jax.ShapeDtypeStruct((heads, rows, 2 * HD), bf16),
         ),
-        in_specs=[pl.BlockSpec(memory_space=pltpu.SMEM), vmem] + [anywhere] * 4,
+        in_specs=[pinned] * 6,
         out_specs=(vmem, vmem),
         scratch_shapes=[
+            pltpu.SMEM((NBR, neighbours.shape[0]), jnp.int32),
+            pltpu.VMEM((heads, rows), f32),
             pltpu.VMEM((tokens, width), bf16),
             pltpu.VMEM((tokens, width), bf16),
             pltpu.VMEM((heads, rows, 2 * HD), bf16),
@@ -436,18 +444,23 @@
             dma((tiles,)),
             dma((tiles,)),
             dma((tiles,)),
-            dma((2 + tiles,)),
+            dma((4 + tiles,)),
         ],
         compiler_params=pltpu.CompilerParams(
             collective_id=0, has_side_effects=True, vmem_limit_bytes=48 * 1024 * 1024
         ),
     )(
-        jnp.transpose(neighbours),
-        log_totals.reshape(heads, rows),
-        upstream.reshape(tokens, width),
-        queries.reshape(tokens, width),
-        attention_out.reshape(tokens, width),
-        keys_values.reshape(heads, rows, 2 * HD),
+        *[
+            pltpu.with_memory_space_constraint(operand, pltpu.HBM)
+            for operand in (
+                jnp.transpose(neighbours),
+                log_totals.reshape(heads, rows),
+                upstream.reshape(tokens, width),
+                queries.reshape(tokens, width),
+                attention_out.reshape(tokens, width),
+                keys_values.reshape(heads, rows, 2 * HD),
+            )
+        ]
     )
     query_grad = jnp.transpose(query_turned, (0, 2, 1)).reshape(1, 1, heads, rows, HD)
     return query_grad, cache_grad.reshape(1, 1, heads, rows, 2 * HD)

time: 47.3 us -> 41 us (0.87)
  local copies, waits for them, and re-layouts: 7.13 us -> 1.63 us
  Pallas kernels: 39.2 us -> 38.6 us
    unnamed x14 -> x2, local copies, waits for them, and re-layouts: 7.13 us -> 1.63 us
    pallas_call x1, Pallas kernels: 39.2 us -> 38.6 us  [fused_body(): pl.pallas_call(fused_kernel, out_shape=(jax.ShapeDtypeStruct((heads, HD,...]
where the time goes in v2:
time: 41 us; the launch traced here: 40.9 us
  Pallas kernels  38.6 us (94%)
  local copies, waits for them, and re-layouts  1.63 us (4%)
  between operations  0.64 us (2%)
    pallas_call x1, Pallas kernels, fused_body(): pl.pallas_call(fused_kernel, out_shape=(jax.ShapeDtypeStruct((heads, HD,...  38.6 us
    unnamed x2, local copies, waits for them, and re-layouts  1.63 us

profile of v2, /device:TPU:0, one launch (start us, length us, event | category | flops | bytes accessed | tf_op | source)
XLA Modules:
  0.0 40.9 jit_solution(3223017534652218072)
XLA Ops:
  0.6 38.6 %shard_map.77 = (bf16[8,64,384]{2,1,0:T(8,128)(2,1)S(1)}, bf16[8,384,128]{2,1,0:T(8,128)(2,1)S(1)}) custom-call(s32[7,12]{1,0:T(8,128)} %bitcast.17, f32[8,384]{1,0:T(8,128)} %bitcast.16, bf16[96,2048]{1,0:T(8,128)(2,1)} %bitcast.13, bf16[96,2048]{1,0:T(8,128)(2,1)} %bitcast.14, bf16[96,2048]{1,0:T(8,128)(2,1)} %bitcast.15, bf16[8,384,128]{2,1,0:T(8,128)(2,1)} %bitcast.12), custom_call_target="tpu_custom_call" | custom-call | tf_op jit(solution)/shard_map/pallas_call | solution.py:409
  39.2 0.7 %copy.10 = bf16[1,1,8,384,64]{3,4,2,1,0:T(8,128)(2,1)} copy(bf16[1,1,8,384,64]{3,4,2,1,0:T(8,128)(2,1)S(1)} %bitcast.11) | data formatting | bytes 786432
  40.0 0.9 %copy.11 = bf16[1,1,8,384,128]{4,3,2,1,0:T(8,128)(2,1)} copy(bf16[1,1,8,384,128]{4,3,2,1,0:T(8,128)(2,1)S(1)} %bitcast.10) | data formatting | bytes 1572864

commit v3 on v2

--- a/solution.py
+++ b/solution.py
@@ -166,7 +166,7 @@
 
 def fused_kernel(
     neigh_hbm, norm_hbm, up_ref, query_ref, out_ref, cache_ref, dq_ref, dkv_ref,
-    neigh_ref, norm_ref, inc, outs, kv, halo, qbuf, gbuf, dsend, dgot, acc, acc_kv, back_out, back_in, bias_own, bias_halo, rows_aux,
+    neigh_ref, norm_ref, inc, outs, kv, halo, qbuf, gbuf, dsend, dgot, acc, acc_kv, back_out, back_in, bias_own, bias_halo, rows_aux, joint,
     up_send, up_recv, q_send, q_recv, g_send, g_recv, d_send, d_recv, h_send, h_recv, b_send, b_recv, local_sem,
 ):
     n_pipe, n_seq = lax.axis_size("pipe"), lax.axis_size("seq")
@@ -262,7 +262,8 @@
     for tile in range(tiles):
         for dest in range(n_seq):
             up_copy(tile, dest).start()
-        h_copy(tile).start()
+        if tile == 0:
+            h_copy(tile).start()
         if tile < 2:
             for step in range(1, n_seq):
                 q_copy(tile, step).start()
@@ -278,6 +279,8 @@
             up_copy(tile, dest).wait_recv()
         for step in range(1, n_seq):
             g_copy(tile, step).start()
+        if tile + 1 < tiles:
+            h_copy(tile + 1).start()
         if tile + 2 < tiles:
             for step in range(1, n_seq):
                 q_copy(tile + 2, step).start()
@@ -317,34 +320,38 @@
         rows_aux[head, 1:2, :] = delta[head : head + 1]
 
     inv_root = HD ** (-0.5)
-
-    def block_terms(keys, values, q_rows, g_rows, bias, norm_row, delta_row):
-        count = keys.shape[0] // BLK
-        keys = keys * jnp.bfloat16(inv_root)
-        scores = dot_f32(keys, q_rows, NT)
+    key_lane = lax.broadcasted_iota(jnp.int32, (1, 2 * HD), 1) < HD
+    lane_scale = jnp.where(key_lane, inv_root, 1.0)
+    lane_scale_half = lane_scale.astype(jnp.bfloat16)
+
+    def block_terms(cache_rows, both_rows, bias, norm_row, delta_row):
+        count, width_here = cache_rows.shape[0] // BLK, delta_row.shape[1]
+        scaled = cache_rows * lane_scale_half
+        products = dot_f32(scaled, both_rows, NT)
+        scores = products[:, :width_here].reshape(count, BLK, width_here)
         shift = bias[:count] - norm_row
-        scores = scores.reshape(count, BLK, scores.shape[1]) + shift[:, None, :]
-        weights = jnp.exp(scores).reshape(keys.shape[0], scores.shape[2])
-        grad_weights = dot_f32(values, g_rows, NT)
-        grad_scores = (weights * (grad_weights - delta_row)).astype(jnp.bfloat16)
-        key_part = dot_f32(grad_scores, q_rows) * inv_root
-        value_part = dot_f32(weights.astype(jnp.bfloat16), g_rows)
-        query_part = dot_f32(keys, grad_scores, TN)
-        return query_part, jnp.concatenate([key_part, value_part], axis=1)
+        weights = jnp.exp(scores + shift[:, None, :]).reshape(count * BLK, width_here)
+        grad_scores = (weights * (products[:, width_here:] - delta_row)).astype(jnp.bfloat16)
+        joined = jnp.concatenate([grad_scores, weights.astype(jnp.bfloat16)], axis=1)
+        cache_part = dot_f32(joined, both_rows) * lane_scale
+        query_part = dot_f32(scaled[:, :HD], grad_scores, TN)
+        return query_part, cache_part
 
     def one_tile(tile, carry):
         for step in range(1, n_seq):
             q_copy(tile, step).wait_recv()
             g_copy(tile, step).wait_recv()
+        blank = jnp.zeros((rows, HD), jnp.bfloat16)
+        for inner in range(PER_TILE):
+            lanes = slice(inner * HD, (inner + 1) * HD)
+            joint[inner, 0] = jnp.concatenate([qbuf[tile, :, lanes], blank], axis=1)
+            joint[inner, 1] = jnp.concatenate([blank, gbuf[tile, :, lanes]], axis=1)
         h_copy(tile).wait_recv()
         for inner in range(PER_TILE):
             head = tile * PER_TILE + inner
-            lanes = slice(inner * HD, (inner + 1) * HD)
             query_part, cache_part = block_terms(
-                halo[head, :, :HD],
-                halo[head, :, HD:],
-                qbuf[tile, pl.ds(window, span), lanes],
-                gbuf[tile, pl.ds(window, span), lanes],
+                halo[head],
+                joint[inner, :, pl.ds(window, span), :].reshape(2 * span, LANES),
                 bias_halo[:, pl.ds(window, span)],
                 rows_aux[head, 0:1, pl.ds(window, span)],
                 rows_aux[head, 1:2, pl.ds(window, span)],
@@ -357,12 +364,9 @@
         b_copy(tile).start()
         for inner in range(PER_TILE):
             head = tile * PER_TILE + inner
-            lanes = slice(inner * HD, (inner + 1) * HD)
             query_part, cache_part = block_terms(
-                kv[head, :, :HD],
-                kv[head, :, HD:],
-                qbuf[tile, :, lanes],
-                gbuf[tile, :, lanes],
+                kv[head],
+                joint[inner].reshape(2 * rows, LANES),
                 bias_own[...],
                 rows_aux[head, 0:1, :],
                 rows_aux[head, 1:2, :],
@@ -432,6 +436,7 @@
             pltpu.VMEM((blocks_pad, rows), f32),
             pltpu.VMEM((8, rows), f32),
             pltpu.VMEM((heads, 8, rows), f32),
+            pltpu.VMEM((PER_TILE, 2, rows, LANES), bf16),
             dma((tiles, n_seq)),
             dma((tiles, n_seq)),
             dma((tiles, n_seq - 1)),

time: 41 us -> 41.1 us (level)
  no operation moved by 1% of the time
where the time goes in v3:
time: 41.1 us; the launch traced here: 41 us
  Pallas kernels  38.7 us (94%)
  local copies, waits for them, and re-layouts  1.63 us (4%)
  between operations  0.64 us (2%)
    pallas_call x1, Pallas kernels, fused_body(): pl.pallas_call(fused_kernel, out_shape=(jax.ShapeDtypeStruct((heads, HD,...  38.7 us
    unnamed x2, local copies, waits for them, and re-layouts  1.63 us

profile of v3, /device:TPU:0, one launch (start us, length us, event | category | flops | bytes accessed | tf_op | source)
XLA Modules:
  0.0 41.0 jit_solution(11220617148574604837)
XLA Ops:
  0.6 38.7 %shard_map.77 = (bf16[8,64,384]{2,1,0:T(8,128)(2,1)S(1)}, bf16[8,384,128]{2,1,0:T(8,128)(2,1)S(1)}) custom-call(s32[7,12]{1,0:T(8,128)} %bitcast.17, f32[8,384]{1,0:T(8,128)} %bitcast.16, bf16[96,2048]{1,0:T(8,128)(2,1)} %bitcast.13, bf16[96,2048]{1,0:T(8,128)(2,1)} %bitcast.14, bf16[96,2048]{1,0:T(8,128)(2,1)} %bitcast.15, bf16[8,384,128]{2,1,0:T(8,128)(2,1)} %bitcast.12), custom_call_target="tpu_custom_call" | custom-call | tf_op jit(solution)/shard_map/pallas_call | solution.py:413
  39.4 0.7 %copy.10 = bf16[1,1,8,384,64]{3,4,2,1,0:T(8,128)(2,1)} copy(bf16[1,1,8,384,64]{3,4,2,1,0:T(8,128)(2,1)S(1)} %bitcast.11) | data formatting | bytes 786432
  40.1 0.9 %copy.11 = bf16[1,1,8,384,128]{4,3,2,1,0:T(8,128)(2,1)} copy(bf16[1,1,8,384,128]{4,3,2,1,0:T(8,128)(2,1)S(1)} %bitcast.10) | data formatting | bytes 1572864

commit v4 on v3

--- a/solution.py
+++ b/solution.py
@@ -259,14 +259,22 @@
         pl.semaphore_signal(barrier, inc=1, device_id={"seq": peer(step)}, device_id_type=MESH)
     pl.semaphore_wait(barrier, n_seq + 1)
 
-    for tile in range(tiles):
+    def send_up(tile):
         for dest in range(n_seq):
             up_copy(tile, dest).start()
-        if tile == 0:
-            h_copy(tile).start()
-        if tile < 2:
-            for step in range(1, n_seq):
-                q_copy(tile, step).start()
+
+    def send_q(tile):
+        for step in range(1, n_seq):
+            q_copy(tile, step).start()
+
+    def send_g(tile):
+        for step in range(1, n_seq):
+            g_copy(tile, step).start()
+
+    send_up(0)
+    send_q(0)
+    h_copy(0).start()
+    send_up(1)
 
     neigh_local.wait()
     first_row = tp * blocks_here
@@ -277,13 +285,13 @@
     for tile in range(tiles):
         for dest in range(n_seq):
             up_copy(tile, dest).wait_recv()
-        for step in range(1, n_seq):
-            g_copy(tile, step).start()
-        if tile + 1 < tiles:
-            h_copy(tile + 1).start()
         if tile + 2 < tiles:
-            for step in range(1, n_seq):
-                q_copy(tile + 2, step).start()
+            send_up(tile + 2)
+        if tile < 2:
+            send_g(tile)
+        if tile == 0:
+            send_q(1)
+            h_copy(1).start()
 
     out_local.wait()
     picks = (
@@ -337,10 +345,24 @@
         query_part = dot_f32(scaled[:, :HD], grad_scores, TN)
         return query_part, cache_part
 
+    def finish(tile):
+        b_copy(tile).wait_recv()
+        for inner in range(PER_TILE):
+            head = tile * PER_TILE + inner
+            acc_kv[head, pl.ds(window, span), :] += back_in[head].astype(jnp.float32)
+            dkv_ref[head] = acc_kv[head].astype(jnp.bfloat16)
+
     def one_tile(tile, carry):
         for step in range(1, n_seq):
             q_copy(tile, step).wait_recv()
             g_copy(tile, step).wait_recv()
+
+        @pl.when(tile + 2 < tiles)
+        def _():
+            send_q(tile + 2)
+            send_g(tile + 2)
+            h_copy(tile + 2).start()
+
         blank = jnp.zeros((rows, HD), jnp.bfloat16)
         for inner in range(PER_TILE):
             lanes = slice(inner * HD, (inner + 1) * HD)
@@ -373,19 +395,15 @@
             )
             dq_ref[head] = (acc[head] + query_part).astype(jnp.bfloat16)
             acc_kv[head] = cache_part
+        @pl.when(tile >= 2)
+        def _():
+            finish(tile - 2)
+
         return carry
 
     lax.fori_loop(0, tiles, one_tile, 0)
-
-    def finish(tile, carry):
-        b_copy(tile).wait_recv()
-        for inner in range(PER_TILE):
-            head = tile * PER_TILE + inner
-            acc_kv[head, pl.ds(window, span), :] += back_in[head].astype(jnp.float32)
-            dkv_ref[head] = acc_kv[head].astype(jnp.bfloat16)
-        return carry
-
-    lax.fori_loop(0, tiles, finish, 0)
+    finish(tiles - 2)
+    finish(tiles - 1)
 
     for tile in range(tiles):
         for dest in range(n_seq):

time: 41.1 us -> 38 us (0.925)
  Pallas kernels: 38.7 us -> 35.6 us
    pallas_call x1, Pallas kernels: 38.7 us -> 35.6 us  [fused_body(): pl.pallas_call(fused_kernel, out_shape=(jax.ShapeDtypeStruct((heads, HD,...]
where the time goes in v4:
time: 38 us; the launch traced here: 37.9 us
  Pallas kernels  35.6 us (94%)
  local copies, waits for them, and re-layouts  1.63 us (4%)
  between operations  0.64 us (2%)
    pallas_call x1, Pallas kernels, fused_body(): pl.pallas_call(fused_kernel, out_shape=(jax.ShapeDtypeStruct((heads, HD,...  35.6 us
    unnamed x2, local copies, waits for them, and re-layouts  1.63 us

profile of v4, /device:TPU:0, one launch (start us, length us, event | category | flops | bytes accessed | tf_op | source)
XLA Modules:
  0.0 37.9 jit_solution(6321822273219779771)
XLA Ops:
  0.6 35.6 %shard_map.77 = (bf16[8,64,384]{2,1,0:T(8,128)(2,1)S(1)}, bf16[8,384,128]{2,1,0:T(8,128)(2,1)S(1)}) custom-call(s32[7,12]{1,0:T(8,128)} %bitcast.17, f32[8,384]{1,0:T(8,128)} %bitcast.16, bf16[96,2048]{1,0:T(8,128)(2,1)} %bitcast.13, bf16[96,2048]{1,0:T(8,128)(2,1)} %bitcast.14, bf16[96,2048]{1,0:T(8,128)(2,1)} %bitcast.15, bf16[8,384,128]{2,1,0:T(8,128)(2,1)} %bitcast.12), custom_call_target="tpu_custom_call" | custom-call | tf_op jit(solution)/shard_map/pallas_call | solution.py:431
  36.3 0.7 %copy.10 = bf16[1,1,8,384,64]{3,4,2,1,0:T(8,128)(2,1)} copy(bf16[1,1,8,384,64]{3,4,2,1,0:T(8,128)(2,1)S(1)} %bitcast.11) | data formatting | bytes 786432
  37.0 0.9 %copy.11 = bf16[1,1,8,384,128]{4,3,2,1,0:T(8,128)(2,1)} copy(bf16[1,1,8,384,128]{4,3,2,1,0:T(8,128)(2,1)S(1)} %bitcast.10) | data formatting | bytes 1572864

commit v5 on v4

--- a/solution.py
+++ b/solution.py
@@ -139,7 +139,6 @@
 PER_TILE = LANES // HD
 ABSENT = -1e30
 NT = (((1,), (1,)), ((), ()))
-TN = (((0,), (0,)), ((), ()))
 
 
 def dot_f32(left, right, dims=(((1,), (0,)), ((), ()))):
@@ -166,7 +165,7 @@
 
 def fused_kernel(
     neigh_hbm, norm_hbm, up_ref, query_ref, out_ref, cache_ref, dq_ref, dkv_ref,
-    neigh_ref, norm_ref, inc, outs, kv, halo, qbuf, gbuf, dsend, dgot, acc, acc_kv, back_out, back_in, bias_own, bias_halo, rows_aux, joint,
+    neigh_ref, norm_ref, inc, outs, kv, halo, qbuf, gbuf, dsend, dgot, acc, acc_kv, back_out, back_in, bias_own, bias_halo, rows_aux, joint, turned, key_turned,
     up_send, up_recv, q_send, q_recv, g_send, g_recv, d_send, d_recv, h_send, h_recv, b_send, b_recv, local_sem,
 ):
     n_pipe, n_seq = lax.axis_size("pipe"), lax.axis_size("seq")
@@ -180,6 +179,7 @@
     below, above = lax.rem(pipe + n_pipe - 1, n_pipe), lax.rem(pipe + 1, n_pipe)
     mate = 1 - tp
     window = pl.multiple_of(mate * (rows - span), LANES)
+    far_window = pl.multiple_of(rows + mate * (rows - span), LANES)
     mine = pl.multiple_of(seq * tokens, 16)
 
     def peer(step):
@@ -282,6 +282,17 @@
     bias_own[...] = listed_bias(neigh_ref, first_row, first_row, bias_own.shape[0], blocks_here)
     bias_halo[...] = listed_bias(neigh_ref, first_row, halo_key, bias_halo.shape[0], blocks_here)
 
+    inv_root = HD ** (-0.5)
+    key_lane = lax.broadcasted_iota(jnp.int32, (1, 2 * HD), 1) < HD
+    lane_scale = jnp.where(key_lane, inv_root, 1.0)
+    lane_scale_half = lane_scale.astype(jnp.bfloat16)
+
+    def prepare(head, carry):
+        scaled = kv[head] * lane_scale_half
+        kv[head] = scaled
+        key_turned[head] = jnp.transpose(scaled)[:HD]
+        return carry
+
     for tile in range(tiles):
         for dest in range(n_seq):
             up_copy(tile, dest).wait_recv()
@@ -292,6 +303,10 @@
         if tile == 0:
             send_q(1)
             h_copy(1).start()
+        if tile == 1:
+            turned[...] = jnp.zeros_like(turned)
+            kv_local.wait()
+            lax.fori_loop(0, heads, prepare, 0)
 
     out_local.wait()
     picks = (
@@ -310,7 +325,6 @@
     dgot[seq] = dsend[seq]
     for tile in range(tiles):
         gbuf[tile, pl.ds(mine, tokens), :] = inc[:, tile_cols(seq, tile)]
-    kv_local.wait()
     for copy in q_local:
         copy.wait()
     for step in range(1, n_seq):
@@ -327,22 +341,16 @@
         rows_aux[head, 0:1, :] = norm[head : head + 1]
         rows_aux[head, 1:2, :] = delta[head : head + 1]
 
-    inv_root = HD ** (-0.5)
-    key_lane = lax.broadcasted_iota(jnp.int32, (1, 2 * HD), 1) < HD
-    lane_scale = jnp.where(key_lane, inv_root, 1.0)
-    lane_scale_half = lane_scale.astype(jnp.bfloat16)
-
-    def block_terms(cache_rows, both_rows, bias, norm_row, delta_row):
-        count, width_here = cache_rows.shape[0] // BLK, delta_row.shape[1]
-        scaled = cache_rows * lane_scale_half
-        products = dot_f32(scaled, both_rows, NT)
+    def block_terms(scaled, keys_turned, both_rows, both_turned, bias, norm_row, delta_row):
+        count, width_here = scaled.shape[0] // BLK, delta_row.shape[1]
+        products = dot_f32(scaled, both_turned)
         scores = products[:, :width_here].reshape(count, BLK, width_here)
         shift = bias[:count] - norm_row
         weights = jnp.exp(scores + shift[:, None, :]).reshape(count * BLK, width_here)
         grad_scores = (weights * (products[:, width_here:] - delta_row)).astype(jnp.bfloat16)
         joined = jnp.concatenate([grad_scores, weights.astype(jnp.bfloat16)], axis=1)
         cache_part = dot_f32(joined, both_rows) * lane_scale
-        query_part = dot_f32(scaled[:, :HD], grad_scores, TN)
+        query_part = dot_f32(keys_turned, grad_scores)
         return query_part, cache_part
 
     def finish(tile):
@@ -364,16 +372,25 @@
             h_copy(tile + 2).start()
 
         blank = jnp.zeros((rows, HD), jnp.bfloat16)
+        q_turned = jnp.transpose(qbuf[tile])
+        g_turned = jnp.transpose(gbuf[tile])
         for inner in range(PER_TILE):
             lanes = slice(inner * HD, (inner + 1) * HD)
             joint[inner, 0] = jnp.concatenate([qbuf[tile, :, lanes], blank], axis=1)
             joint[inner, 1] = jnp.concatenate([blank, gbuf[tile, :, lanes]], axis=1)
+            turned[inner, :HD, :rows] = q_turned[lanes]
+            turned[inner, HD:, rows:] = g_turned[lanes]
         h_copy(tile).wait_recv()
         for inner in range(PER_TILE):
             head = tile * PER_TILE + inner
+            scaled = halo[head] * lane_scale_half
             query_part, cache_part = block_terms(
-                halo[head],
+                scaled,
+                jnp.transpose(scaled)[:HD],
                 joint[inner, :, pl.ds(window, span), :].reshape(2 * span, LANES),
+                jnp.concatenate(
+                    [turned[inner, :, pl.ds(window, span)], turned[inner, :, pl.ds(far_window, span)]], axis=1
+                ),
                 bias_halo[:, pl.ds(window, span)],
                 rows_aux[head, 0:1, pl.ds(window, span)],
                 rows_aux[head, 1:2, pl.ds(window, span)],
@@ -388,7 +405,9 @@
             head = tile * PER_TILE + inner
             query_part, cache_part = block_terms(
                 kv[head],
+                key_turned[head],
                 joint[inner].reshape(2 * rows, LANES),
+                turned[inner],
                 bias_own[...],
                 rows_aux[head, 0:1, :],
                 rows_aux[head, 1:2, :],
@@ -455,6 +474,8 @@
             pltpu.VMEM((8, rows), f32),
             pltpu.VMEM((heads, 8, rows), f32),
             pltpu.VMEM((PER_TILE, 2, rows, LANES), bf16),
+            pltpu.VMEM((PER_TILE, 2 * HD, 2 * rows), bf16),
+            pltpu.VMEM((heads, HD, rows), bf16),
             dma((tiles, n_seq)),
             dma((tiles, n_seq)),
             dma((tiles, n_seq - 1)),

time: 38 us -> 38 us (level)
  no operation moved by 1% of the time
where the time goes in v5:
time: 38 us; the launch traced here: 37.9 us
  Pallas kernels  35.6 us (94%)
  local copies, waits for them, and re-layouts  1.63 us (4%)
  between operations  0.64 us (2%)
    pallas_call x1, Pallas kernels, fused_body(): pl.pallas_call(fused_kernel, out_shape=(jax.ShapeDtypeStruct((heads, HD,...  35.6 us
    unnamed x2, local copies, waits for them, and re-layouts  1.63 us

profile of v5, /device:TPU:0, one launch (start us, length us, event | category | flops | bytes accessed | tf_op | source)
XLA Modules:
  0.0 37.9 jit_solution(525520320411289812)
XLA Ops:
  0.6 35.6 %shard_map.77 = (bf16[8,64,384]{2,1,0:T(8,128)(2,1)S(1)}, bf16[8,384,128]{2,1,0:T(8,128)(2,1)S(1)}) custom-call(s32[7,12]{1,0:T(8,128)} %bitcast.17, f32[8,384]{1,0:T(8,128)} %bitcast.16, bf16[96,2048]{1,0:T(8,128)(2,1)} %bitcast.13, bf16[96,2048]{1,0:T(8,128)(2,1)} %bitcast.14, bf16[96,2048]{1,0:T(8,128)(2,1)} %bitcast.15, bf16[8,384,128]{2,1,0:T(8,128)(2,1)} %bitcast.12), custom_call_target="tpu_custom_call" | custom-call | tf_op jit(solution)/shard_map/pallas_call | solution.py:450
  36.3 0.7 %copy.10 = bf16[1,1,8,384,64]{3,4,2,1,0:T(8,128)(2,1)} copy(bf16[1,1,8,384,64]{3,4,2,1,0:T(8,128)(2,1)S(1)} %bitcast.11) | data formatting | bytes 786432
  37.0 0.9 %copy.11 = bf16[1,1,8,384,128]{4,3,2,1,0:T(8,128)(2,1)} copy(bf16[1,1,8,384,128]{4,3,2,1,0:T(8,128)(2,1)S(1)} %bitcast.10) | data formatting | bytes 1572864

commit v6 on v5

--- a/solution.py
+++ b/solution.py
@@ -183,6 +183,8 @@
     mine = pl.multiple_of(seq * tokens, 16)
 
     def peer(step):
+        if n_seq == 4:
+            return (lax.rem(seq + 2, 4), 3 - seq, seq + 1 - 2 * lax.rem(seq, 2))[step - 1]
         return lax.rem(seq + step, n_seq)
 
     def tile_cols(dest, tile):
@@ -227,11 +229,10 @@
             device_id={"tp": mate}, device_id_type=MESH,
         )
 
-    def b_copy(tile):
-        pair = pl.ds(tile * PER_TILE, PER_TILE)
+    def b_copy(head):
         return pltpu.make_async_remote_copy(
-            src_ref=back_out.at[pair], dst_ref=back_in.at[pair],
-            send_sem=b_send.at[tile], recv_sem=b_recv.at[tile],
+            src_ref=back_out.at[head], dst_ref=back_in.at[head],
+            send_sem=b_send.at[head], recv_sem=b_recv.at[head],
             device_id={"tp": mate}, device_id_type=MESH,
         )
 
@@ -300,9 +301,9 @@
             send_up(tile + 2)
         if tile < 2:
             send_g(tile)
-        if tile == 0:
-            send_q(1)
-            h_copy(1).start()
+            send_q(tile + 1)
+        if tile + 1 < tiles:
+            h_copy(tile + 1).start()
         if tile == 1:
             turned[...] = jnp.zeros_like(turned)
             kv_local.wait()
@@ -354,9 +355,9 @@
         return query_part, cache_part
 
     def finish(tile):
-        b_copy(tile).wait_recv()
         for inner in range(PER_TILE):
             head = tile * PER_TILE + inner
+            b_copy(head).wait_recv()
             acc_kv[head, pl.ds(window, span), :] += back_in[head].astype(jnp.float32)
             dkv_ref[head] = acc_kv[head].astype(jnp.bfloat16)
 
@@ -367,9 +368,11 @@
 
         @pl.when(tile + 2 < tiles)
         def _():
-            send_q(tile + 2)
             send_g(tile + 2)
-            h_copy(tile + 2).start()
+
+        @pl.when(tile + 3 < tiles)
+        def _():
+            send_q(tile + 3)
 
         blank = jnp.zeros((rows, HD), jnp.bfloat16)
         q_turned = jnp.transpose(qbuf[tile])
@@ -396,11 +399,11 @@
                 rows_aux[head, 1:2, pl.ds(window, span)],
             )
             back_out[head] = cache_part.astype(jnp.bfloat16)
+            b_copy(head).start()
             acc[head, :, pl.ds(window, span)] = query_part
             acc[head, :, pl.ds(pl.multiple_of(tp * span, LANES), rows - span)] = jnp.zeros(
                 (HD, rows - span), jnp.float32
             )
-        b_copy(tile).start()
         for inner in range(PER_TILE):
             head = tile * PER_TILE + inner
             query_part, cache_part = block_terms(
@@ -431,7 +434,8 @@
             q_copy(tile, step).wait_send()
             g_copy(tile, step).wait_send()
         h_copy(tile).wait_send()
-        b_copy(tile).wait_send()
+        for inner in range(PER_TILE):
+            b_copy(tile * PER_TILE + inner).wait_send()
     for step in range(1, n_seq):
         d_copy(step).wait_send()
 
@@ -486,8 +490,8 @@
             dma((n_seq - 1,)),
             dma((tiles,)),
             dma((tiles,)),
-            dma((tiles,)),
-            dma((tiles,)),
+            dma((heads,)),
+            dma((heads,)),
             dma((4 + tiles,)),
         ],
         compiler_params=pltpu.CompilerParams(

time: 38 us -> 34.8 us (0.916)
  Pallas kernels: 35.6 us -> 32.4 us
    pallas_call x1, Pallas kernels: 35.6 us -> 32.4 us  [fused_body(): pl.pallas_call(fused_kernel, out_shape=(jax.ShapeDtypeStruct((heads, HD,...]
where the time goes in v6:
time: 34.8 us; the launch traced here: 34.7 us
  Pallas kernels  32.4 us (93%)
  local copies, waits for them, and re-layouts  1.63 us (5%)
  between operations  0.64 us (2%)
    pallas_call x1, Pallas kernels, fused_body(): pl.pallas_call(fused_kernel, out_shape=(jax.ShapeDtypeStruct((heads, HD,...  32.4 us
    unnamed x2, local copies, waits for them, and re-layouts  1.63 us

profile of v6, /device:TPU:0, one launch (start us, length us, event | category | flops | bytes accessed | tf_op | source)
XLA Modules:
  0.0 34.7 jit_solution(4210205384866729623)
XLA Ops:
  0.6 32.4 %shard_map.77 = (bf16[8,64,384]{2,1,0:T(8,128)(2,1)S(1)}, bf16[8,384,128]{2,1,0:T(8,128)(2,1)S(1)}) custom-call(s32[7,12]{1,0:T(8,128)} %bitcast.17, f32[8,384]{1,0:T(8,128)} %bitcast.16, bf16[96,2048]{1,0:T(8,128)(2,1)} %bitcast.13, bf16[96,2048]{1,0:T(8,128)(2,1)} %bitcast.14, bf16[96,2048]{1,0:T(8,128)(2,1)} %bitcast.15, bf16[8,384,128]{2,1,0:T(8,128)(2,1)} %bitcast.12), custom_call_target="tpu_custom_call" | custom-call | tf_op jit(solution)/shard_map/pallas_call | solution.py:454
  33.0 0.7 %copy.10 = bf16[1,1,8,384,64]{3,4,2,1,0:T(8,128)(2,1)} copy(bf16[1,1,8,384,64]{3,4,2,1,0:T(8,128)(2,1)S(1)} %bitcast.11) | data formatting | bytes 786432
  33.8 0.9 %copy.11 = bf16[1,1,8,384,128]{4,3,2,1,0:T(8,128)(2,1)} copy(bf16[1,1,8,384,128]{4,3,2,1,0:T(8,128)(2,1)S(1)} %bitcast.10) | data formatting | bytes 1572864

commit v7 on v6

--- a/solution.py
+++ b/solution.py
@@ -272,8 +272,9 @@
         for step in range(1, n_seq):
             g_copy(tile, step).start()
 
+    send_q(0)
     send_up(0)
-    send_q(0)
+    send_q(1)
     h_copy(0).start()
     send_up(1)
 
@@ -301,6 +302,7 @@
             send_up(tile + 2)
         if tile < 2:
             send_g(tile)
+        if tile == 1:
             send_q(tile + 1)
         if tile + 1 < tiles:
             h_copy(tile + 1).start()

time: 34.8 us -> 34.7 us (level)
  no operation moved by 1% of the time
where the time goes in v7:
time: 34.7 us; the launch traced here: 34.5 us
  Pallas kernels  32.3 us (93%)
  local copies, waits for them, and re-layouts  1.63 us (5%)
  between operations  0.64 us (2%)
    pallas_call x1, Pallas kernels, fused_body(): pl.pallas_call(fused_kernel, out_shape=(jax.ShapeDtypeStruct((heads, HD,...  32.3 us
    unnamed x2, local copies, waits for them, and re-layouts  1.63 us

profile of v7, /device:TPU:0, one launch (start us, length us, event | category | flops | bytes accessed | tf_op | source)
XLA Modules:
  0.0 34.5 jit_solution(15659720671610829605)
XLA Ops:
  0.6 32.3 %shard_map.77 = (bf16[8,64,384]{2,1,0:T(8,128)(2,1)S(1)}, bf16[8,384,128]{2,1,0:T(8,128)(2,1)S(1)}) custom-call(s32[7,12]{1,0:T(8,128)} %bitcast.17, f32[8,384]{1,0:T(8,128)} %bitcast.16, bf16[96,2048]{1,0:T(8,128)(2,1)} %bitcast.13, bf16[96,2048]{1,0:T(8,128)(2,1)} %bitcast.14, bf16[96,2048]{1,0:T(8,128)(2,1)} %bitcast.15, bf16[8,384,128]{2,1,0:T(8,128)(2,1)} %bitcast.12), custom_call_target="tpu_custom_call" | custom-call | tf_op jit(solution)/shard_map/pallas_call | solution.py:456
  32.9 0.7 %copy.10 = bf16[1,1,8,384,64]{3,4,2,1,0:T(8,128)(2,1)} copy(bf16[1,1,8,384,64]{3,4,2,1,0:T(8,128)(2,1)S(1)} %bitcast.11) | data formatting | bytes 786432
  33.7 0.9 %copy.11 = bf16[1,1,8,384,128]{4,3,2,1,0:T(8,128)(2,1)} copy(bf16[1,1,8,384,128]{4,3,2,1,0:T(8,128)(2,1)S(1)} %bitcast.10) | data formatting | bytes 1572864

commit v8 on v7

--- a/solution.py
+++ b/solution.py
@@ -300,7 +300,7 @@
             up_copy(tile, dest).wait_recv()
         if tile + 2 < tiles:
             send_up(tile + 2)
-        if tile < 2:
+        if tile < 3:
             send_g(tile)
         if tile == 1:
             send_q(tile + 1)
@@ -368,13 +368,10 @@
             q_copy(tile, step).wait_recv()
             g_copy(tile, step).wait_recv()
 
-        @pl.when(tile + 2 < tiles)
-        def _():
-            send_g(tile + 2)
-
         @pl.when(tile + 3 < tiles)
         def _():
             send_q(tile + 3)
+            send_g(tile + 3)
 
         blank = jnp.zeros((rows, HD), jnp.bfloat16)
         q_turned = jnp.transpose(qbuf[tile])

time: 34.7 us -> 36.8 us (1.061)
  Pallas kernels: 32.3 us -> 34.4 us
    pallas_call x1, Pallas kernels: 32.3 us -> 34.4 us  [fused_body(): pl.pallas_call(fused_kernel, out_shape=(jax.ShapeDtypeStruct((heads, HD,...]
where the time goes in v8:
time: 36.8 us; the launch traced here: 36.7 us
  Pallas kernels  34.4 us (93%)
  local copies, waits for them, and re-layouts  1.63 us (4%)
  between operations  0.64 us (2%)
    pallas_call x1, Pallas kernels, fused_body(): pl.pallas_call(fused_kernel, out_shape=(jax.ShapeDtypeStruct((heads, HD,...  34.4 us
    unnamed x2, local copies, waits for them, and re-layouts  1.63 us

profile of v8, /device:TPU:0, one launch (start us, length us, event | category | flops | bytes accessed | tf_op | source)
XLA Modules:
  0.0 36.7 jit_solution(14734209375867054615)
XLA Ops:
  0.6 34.4 %shard_map.77 = (bf16[8,64,384]{2,1,0:T(8,128)(2,1)S(1)}, bf16[8,384,128]{2,1,0:T(8,128)(2,1)S(1)}) custom-call(s32[7,12]{1,0:T(8,128)} %bitcast.17, f32[8,384]{1,0:T(8,128)} %bitcast.16, bf16[96,2048]{1,0:T(8,128)(2,1)} %bitcast.13, bf16[96,2048]{1,0:T(8,128)(2,1)} %bitcast.14, bf16[96,2048]{1,0:T(8,128)(2,1)} %bitcast.15, bf16[8,384,128]{2,1,0:T(8,128)(2,1)} %bitcast.12), custom_call_target="tpu_custom_call" | custom-call | tf_op jit(solution)/shard_map/pallas_call | solution.py:453
  35.0 0.7 %copy.10 = bf16[1,1,8,384,64]{3,4,2,1,0:T(8,128)(2,1)} copy(bf16[1,1,8,384,64]{3,4,2,1,0:T(8,128)(2,1)S(1)} %bitcast.11) | data formatting | bytes 786432
  35.8 0.9 %copy.11 = bf16[1,1,8,384,128]{4,3,2,1,0:T(8,128)(2,1)} copy(bf16[1,1,8,384,128]{4,3,2,1,0:T(8,128)(2,1)S(1)} %bitcast.10) | data formatting | bytes 1572864
